TPU v7x, 32 devices: a whole 2x2x4 slice. The times are simulated.
32 devices in a mesh: rep: 2 (over y), seq: 4 (over x, core), head: 4 (over z).
Axes of the slice: x: 2, y: 2, z: 4, core: 2. Of those that a mesh axis runs over, the one named last changes fastest.
Arguments:
- queries: bfloat16 [2048, 4096], P(('rep', 'seq', 'head')), parts along dimension 0, may hold values from -6 to 6
- key_rows: bfloat16 [2048, 4096], P(('rep', 'seq', 'head')), parts along dimension 0, may hold values from -6 to 6
- value_rows: bfloat16 [2048, 4096], P(('rep', 'seq', 'head')), parts along dimension 0, may hold values from -6 to 6
- out_grad: bfloat16 [2048, 4096], P(('rep', 'seq', 'head')), parts along dimension 0, may hold values from -6 to 6
Outputs:
- attended: bfloat16 [2048, 4096], P(('rep', 'seq', 'head')), parts along dimension 0
- query_grad: bfloat16 [2048, 4096], P(('rep', 'seq', 'head')), parts along dimension 0
- key_grad: bfloat16 [2048, 4096], P(('rep', 'seq', 'head')), parts along dimension 0
- value_grad: bfloat16 [2048, 4096], P(('rep', 'seq', 'head')), parts along dimension 0
There are 2 independent parts, one for each index of `rep`. A program takes and returns all parts, laid end to end along the dimension named above; each array names one. Nothing has to cross between parts.
All inputs are finite; a program needn't handle non-finite values.
Results may differ from a plain program's by a relative error of at most 0.0049.
Values may be sent and summed in bfloat16 or wider, within the bound.
A program may use at most 64 MiB of HBM per device.

v0:
```python
import jax
import jax.numpy as jnp
from jax import lax
from jax.sharding import PartitionSpec as P

DH = 128
BLK_MAX = 512


def shards(queries, key_rows, value_rows, out_grad):
    f32 = jnp.float32
    bf16 = jnp.bfloat16
    head_count = lax.axis_size("head")
    tok_count = queries.shape[0]
    local_heads = queries.shape[1] // (head_count * DH)
    seq_rows = tok_count * head_count
    block = min(BLK_MAX, seq_rows)
    block_count = seq_rows // block
    factor = float(DH * seq_rows * lax.axis_size("seq")) ** (-0.5)

    def to_heads(matrix):
        return matrix.reshape(tok_count, head_count, local_heads, DH)

    def per_head(parts):
        heads_here = parts[0].shape[2]
        query_blocks, key_blocks, value_blocks, grad_blocks = (
            item.reshape(block_count, block, heads_here, DH) for item in parts
        )
        kv_state = jnp.einsum(
            "bthd,bthe->bhde", key_blocks, value_blocks, preferred_element_type=f32
        )
        grad_state = jnp.einsum(
            "bthd,bthe->bhde", query_blocks, grad_blocks, preferred_element_type=f32
        )
        empty_state = jnp.zeros((1, heads_here, DH, DH), f32)
        local_prefix = jnp.concatenate([empty_state, jnp.cumsum(kv_state, 0)[:-1]], 0)
        tail_sums = jnp.cumsum(grad_state[::-1], 0)[::-1]
        local_suffix = jnp.concatenate([tail_sums[1:], empty_state], 0)
        kv_total = jnp.sum(kv_state, 0)
        grad_total = jnp.sum(grad_state, 0)
        my_index = lax.axis_index("seq")
        pieces = (
            lax.all_gather(kv_total[None], "seq", axis=0, tiled=True),
            lax.all_gather(grad_total[None], "seq", axis=0, tiled=True),
        )
        count = pieces[0].shape[0]
        index = jnp.arange(count, dtype=jnp.int32)
        below_me = (index < my_index).astype(f32)[:, None, None, None]
        above_me = (index > my_index).astype(f32)[:, None, None, None]
        span_prefix = jnp.sum(pieces[0] * below_me, 0)
        span_suffix = jnp.sum(pieces[1] * above_me, 0)
        prefix = (local_prefix + span_prefix[None]).astype(bf16)
        suffix = (local_suffix + span_suffix[None]).astype(bf16)
        causal = (jnp.arange(block)[:, None] >= jnp.arange(block)[None, :])[None, None]
        scores = jnp.einsum("bthd,bshd->bhts", query_blocks, key_blocks, preferred_element_type=f32)
        scores = jnp.where(causal, scores * factor, 0.0).astype(bf16)
        attended = jnp.einsum("bhts,bshd->bthd", scores, value_blocks, preferred_element_type=f32)
        attended = attended + factor * jnp.einsum(
            "bthd,bhde->bthe", query_blocks, prefix, preferred_element_type=f32
        )
        dscores = jnp.einsum(
            "bthe,bshe->bhts", grad_blocks, value_blocks, preferred_element_type=f32
        )
        dscores = jnp.where(causal, dscores * factor, 0.0).astype(bf16)
        query_grad = jnp.einsum("bhts,bshd->bthd", dscores, key_blocks, preferred_element_type=f32)
        query_grad = query_grad + factor * jnp.einsum(
            "bthe,bhde->bthd", grad_blocks, prefix, preferred_element_type=f32
        )
        key_grad = jnp.einsum("bhts,bthd->bshd", dscores, query_blocks, preferred_element_type=f32)
        key_grad = key_grad + factor * jnp.einsum(
            "bshe,bhde->bshd", value_blocks, suffix, preferred_element_type=f32
        )
        value_grad = jnp.einsum("bhts,bthe->bshe", scores, grad_blocks, preferred_element_type=f32)
        value_grad = value_grad + factor * jnp.einsum(
            "bshd,bhde->bshe", key_blocks, suffix, preferred_element_type=f32
        )
        results = tuple(
            (
                item.astype(bf16).reshape(seq_rows, 1, heads_here, DH)
                for item in (attended, query_grad, key_grad, value_grad)
            )
        )
        return (
            lax.all_to_all(results[0], "head", split_axis=0, concat_axis=1, tiled=True),
            lax.all_to_all(results[1], "head", split_axis=0, concat_axis=1, tiled=True),
            lax.all_to_all(results[2], "head", split_axis=0, concat_axis=1, tiled=True),
            lax.all_to_all(results[3], "head", split_axis=0, concat_axis=1, tiled=True),
        )

    outputs = per_head(
        (
            lax.all_to_all(to_heads(queries), "head", split_axis=1, concat_axis=0, tiled=True),
            lax.all_to_all(to_heads(key_rows), "head", split_axis=1, concat_axis=0, tiled=True),
            lax.all_to_all(to_heads(value_rows), "head", split_axis=1, concat_axis=0, tiled=True),
            lax.all_to_all(to_heads(out_grad), "head", split_axis=1, concat_axis=0, tiled=True),
        )
    )
    return tuple((item.reshape(tok_count, queries.shape[1]) for item in outputs))


def solution(mesh):
    placed = (
        P(("rep", "seq", "head"), None),
        P(("rep", "seq", "head"), None),
        P(("rep", "seq", "head"), None),
        P(("rep", "seq", "head"), None),
    )
    return jax.shard_map(
        shards,
        mesh=mesh,
        in_specs=placed,
        out_specs=(
            P(("rep", "seq", "head"), None),
            P(("rep", "seq", "head"), None),
            P(("rep", "seq", "head"), None),
            P(("rep", "seq", "head"), None),
        ),
        check_vma=False,
    )
```

profile of v0, /device:TPU:0, one launch (start us, length us, event | category | flops | bytes accessed | tf_op | source)
XLA Modules:
  0.0 174.0 jit_solution(1147366358603336593)
XLA Ops:
  7.2 0.0 copy-start.4
  7.2 1.2 copy.85
  8.4 1.0 copy.50
  9.4 6.3 %all-to-all-start.1 = ((bf16[64,4,8,128]{3,0,2,1:T(8,128)(2,1)}), bf16[64,4,8,128]{3,0,2,1:T(8,128)(2,1)S(1)}, u32[]{:S(2)}, u32[]{:S(2)}) async-start(bf16[64,4,8,128]{3,0,2,1:T(8,128)(2,1)} %copy.50), calls=%async_computation.1 | async-start | bytes 1048576 | tf_op jit(solution)/shard_map/all_to_all | solution.py:93
  15.7 0.0 copy-done.4
  15.7 0.1 copy.86
  15.8 1.0 copy.52
  16.8 13.4 %all-to-all-done.1 = bf16[64,4,8,128]{3,0,2,1:T(8,128)(2,1)S(1)} async-done(((bf16[64,4,8,128]{3,0,2,1:T(8,128)(2,1)}), bf16[64,4,8,128]{3,0,2,1:T(8,128)(2,1)S(1)}, u32[]{:S(2)}, u32[]{:S(2)}) %all-to-all-start.1) | async-done | bytes 524320 | tf_op jit(solution)/shard_map/all_to_all | solution.py:93
  30.2 3.5 %all-to-all-start.2 = ((bf16[64,4,8,128]{3,0,2,1:T(8,128)(2,1)}), bf16[64,4,8,128]{3,0,2,1:T(8,128)(2,1)S(1)}, u32[]{:S(2)}, u32[]{:S(2)}) async-start(bf16[64,4,8,128]{3,0,2,1:T(8,128)(2,1)} %copy.52), calls=%async_computation.2 | async-start | bytes 1048576 | tf_op jit(solution)/shard_map/all_to_all | solution.py:94
  33.7 0.0 all-gather.5.cloned.1.call-start
  33.7 0.0 copy-start.5
  33.8 13.9 %all-to-all-done.2 = bf16[64,4,8,128]{3,0,2,1:T(8,128)(2,1)S(1)} async-done(((bf16[64,4,8,128]{3,0,2,1:T(8,128)(2,1)}), bf16[64,4,8,128]{3,0,2,1:T(8,128)(2,1)S(1)}, u32[]{:S(2)}, u32[]{:S(2)}) %all-to-all-start.2) | async-done | bytes 524320 | tf_op jit(solution)/shard_map/all_to_all | solution.py:94
  47.7 1.1 fusion.16
  48.8 0.0 all-gather.5.cloned.1.call-update
  48.8 0.0 copy-done.5
  48.8 0.1 copy.84
  48.9 1.0 copy.48
  49.9 3.5 %all-to-all-start = ((bf16[64,4,8,128]{3,0,2,1:T(8,128)(2,1)}), bf16[64,4,8,128]{3,0,2,1:T(8,128)(2,1)S(1)}, u32[]{:S(2)}, u32[]{:S(2)}) async-start(bf16[64,4,8,128]{3,0,2,1:T(8,128)(2,1)} %copy.48), calls=%async_computation | async-start | bytes 1048576 | tf_op jit(solution)/shard_map/all_to_all | solution.py:92
  53.4 0.0 copy-done.6
  53.4 0.1 copy.87
  53.5 1.0 copy.59
  54.5 12.8 %all-to-all-done = bf16[64,4,8,128]{3,0,2,1:T(8,128)(2,1)S(1)} async-done(((bf16[64,4,8,128]{3,0,2,1:T(8,128)(2,1)}), bf16[64,4,8,128]{3,0,2,1:T(8,128)(2,1)S(1)}, u32[]{:S(2)}, u32[]{:S(2)}) %all-to-all-start) | async-done | bytes 524320 | tf_op jit(solution)/shard_map/all_to_all | solution.py:92
  67.4 3.5 %all-to-all-start.4 = ((bf16[64,4,8,128]{3,0,2,1:T(8,128)(2,1)}), bf16[64,4,8,128]{3,0,2,1:T(8,128)(2,1)S(1)}, u32[]{:S(2)}, u32[]{:S(2)}) async-start(bf16[64,4,8,128]{3,0,2,1:T(8,128)(2,1)} %copy.59), calls=%async_computation.4 | async-start | bytes 1048576 | tf_op jit(solution)/shard_map/all_to_all | solution.py:95
  70.8 0.0 all-gather.7.cloned.1.call-start
  70.9 13.9 %all-to-all-done.4 = bf16[64,4,8,128]{3,0,2,1:T(8,128)(2,1)S(1)} async-done(((bf16[64,4,8,128]{3,0,2,1:T(8,128)(2,1)}), bf16[64,4,8,128]{3,0,2,1:T(8,128)(2,1)S(1)}, u32[]{:S(2)}, u32[]{:S(2)}) %all-to-all-start.4) | async-done | bytes 524320 | tf_op jit(solution)/shard_map/all_to_all | solution.py:95
  84.8 1.1 fusion.17
  86.0 0.0 all-gather.7.cloned.1.call-update
  86.1 0.4 select_convert_fusion.1
  86.5 1.4 convolution_bitcast_fusion.3
  87.9 1.9 %multiply_reduce_fusion.1 = bf16[8,128,128]{2,1,0:T(8,128)(2,1)S(1)} fusion(f32[4,8,128,128]{3,2,1,0:T(8,128)} %bitcast.130, f32[4]{0:T(128)S(1)} %compare_convert_fusion.1), kind=kLoop, calls=%fused_computation.2 | loop fusion | flops 917504 | bytes 2359312 | tf_op jit(solution)/shard_map/reduce_sum | solution.py:50
  89.9 0.0 copy-done.1
  89.9 0.3 fusion.9
  90.2 1.1 copy.57
  91.3 4.1 %all-to-all-start.3 = ((bf16[256,1,8,128]{3,2,1,0:T(8,128)(2,1)}), bf16[256,1,8,128]{3,2,1,0:T(8,128)(2,1)}, u32[]{:S(2)}, u32[]{:S(2)}) async-start(bf16[256,1,8,128]{3,2,1,0:T(8,128)(2,1)} %copy.57), calls=%async_computation.3 | async-start | bytes 1048576 | tf_op jit(solution)/shard_map/all_to_all | solution.py:84
  95.5 1.5 convolution_bitcast_fusion
  96.9 10.9 %all-gather.7.cloned.1.call-done = f32[32,128,128]{2,1,0:T(8,128)} async-done(((f32[8,128,128]{2,1,0:T(8,128)}), f32[32,128,128]{2,1,0:T(8,128)}) %all-gather.7.cloned.1.call-update) | async-done | bytes 2097168 | tf_op jit(solution)/shard_map/all_gather | solution.py:44
  107.9 1.9 %multiply_reduce_fusion = bf16[8,128,128]{2,1,0:T(8,128)(2,1)S(1)} fusion(f32[4,8,128,128]{3,2,1,0:T(8,128)} %bitcast.131, f32[4]{0:T(128)S(1)} %compare_convert_fusion), kind=kLoop, calls=%fused_computation | loop fusion | flops 917504 | bytes 2359312 | tf_op jit(solution)/shard_map/reduce_sum | solution.py:51
  109.7 0.0 copy-start.2
  109.7 0.3 fusion.8
  110.0 0.4 copy-done.2
  110.4 1.1 copy.72
  111.6 0.0 all-to-all-done.3
  111.6 4.6 %all-to-all-start.7 = ((bf16[256,1,8,128]{3,2,1,0:T(8,128)(2,1)}), bf16[256,1,8,128]{3,2,1,0:T(8,128)(2,1)}, u32[]{:S(2)}, u32[]{:S(2)}) async-start(bf16[256,1,8,128]{3,2,1,0:T(8,128)(2,1)} %copy.72), calls=%async_computation.7 | async-start | bytes 1048576 | tf_op jit(solution)/shard_map/all_to_all | solution.py:87
  116.2 0.4 select_convert_fusion
  116.6 0.5 convolution_bitcast_fusion.1
  117.1 0.0 copy-done.3
  117.1 0.3 fusion.10
  117.4 1.1 copy.67
  118.6 12.6 %all-to-all-done.7 = bf16[256,1,8,128]{3,2,1,0:T(8,128)(2,1)} async-done(((bf16[256,1,8,128]{3,2,1,0:T(8,128)(2,1)}), bf16[256,1,8,128]{3,2,1,0:T(8,128)(2,1)}, u32[]{:S(2)}, u32[]{:S(2)}) %all-to-all-start.7) | async-done | bytes 524320 | tf_op jit(solution)/shard_map/all_to_all | solution.py:87
  131.2 3.5 %all-to-all-start.6 = ((bf16[256,1,8,128]{3,2,1,0:T(8,128)(2,1)}), bf16[256,1,8,128]{3,2,1,0:T(8,128)(2,1)S(1)}, u32[]{:S(2)}, u32[]{:S(2)}) async-start(bf16[256,1,8,128]{3,2,1,0:T(8,128)(2,1)} %copy.67), calls=%async_computation.6 | async-start | bytes 1048576 | tf_op jit(solution)/shard_map/all_to_all | solution.py:86
  134.6 0.4 convolution_bitcast_fusion.2
  135.1 0.3 fusion.11
  135.4 1.1 copy.62
  136.5 12.1 %all-to-all-done.6 = bf16[256,1,8,128]{3,2,1,0:T(8,128)(2,1)S(1)} async-done(((bf16[256,1,8,128]{3,2,1,0:T(8,128)(2,1)}), bf16[256,1,8,128]{3,2,1,0:T(8,128)(2,1)S(1)}, u32[]{:S(2)}, u32[]{:S(2)}) %all-to-all-start.6) | async-done | bytes 524320 | tf_op jit(solution)/shard_map/all_to_all | solution.py:86
  148.7 3.5 %all-to-all-start.5 = ((bf16[256,1,8,128]{3,2,1,0:T(8,128)(2,1)}), bf16[256,1,8,128]{3,2,1,0:T(8,128)(2,1)S(1)}, u32[]{:S(2)}, u32[]{:S(2)}) async-start(bf16[256,1,8,128]{3,2,1,0:T(8,128)(2,1)} %copy.62), calls=%async_computation.5 | async-start | bytes 1048576 | tf_op jit(solution)/shard_map/all_to_all | solution.py:85
  152.1 1.1 copy.58
  153.3 1.0 reshape.189
  154.3 1.1 copy.73
  155.4 1.0 reshape.197
  156.4 0.1 copy.68
  156.5 1.0 reshape.195
  157.6 8.5 %all-to-all-done.5 = bf16[256,1,8,128]{3,2,1,0:T(8,128)(2,1)S(1)} async-done(((bf16[256,1,8,128]{3,2,1,0:T(8,128)(2,1)}), bf16[256,1,8,128]{3,2,1,0:T(8,128)(2,1)S(1)}, u32[]{:S(2)}, u32[]{:S(2)}) %all-to-all-start.5) | async-done | bytes 524320 | tf_op jit(solution)/shard_map/all_to_all | solution.py:85
  166.1 0.1 copy.63
  166.2 1.0 reshape.193
  (13 shorter events, 0.2 us)
Async XLA Ops:
  7.2 8.5 %copy-start.4 = (bf16[64,4096]{1,0:T(8,128)(2,1)S(1)}, bf16[64,4096]{1,0:T(8,128)(2,1)}, u32[]{:S(2)}) copy-start(bf16[64,4096]{1,0:T(8,128)(2,1)} %param.6) | copy-start | bytes 1572868
  9.4 20.8 %all-to-all-start.1 = ((bf16[64,4,8,128]{3,0,2,1:T(8,128)(2,1)}), bf16[64,4,8,128]{3,0,2,1:T(8,128)(2,1)S(1)}, u32[]{:S(2)}, u32[]{:S(2)}) async-start(bf16[64,4,8,128]{3,0,2,1:T(8,128)(2,1)} %copy.50), calls=%async_computation.1 | async-start | bytes 1048576 | tf_op jit(solution)/shard_map/all_to_all | solution.py:93
  30.2 17.4 %all-to-all-start.2 = ((bf16[64,4,8,128]{3,0,2,1:T(8,128)(2,1)}), bf16[64,4,8,128]{3,0,2,1:T(8,128)(2,1)S(1)}, u32[]{:S(2)}, u32[]{:S(2)}) async-start(bf16[64,4,8,128]{3,0,2,1:T(8,128)(2,1)} %copy.52), calls=%async_computation.2 | async-start | bytes 1048576 | tf_op jit(solution)/shard_map/all_to_all | solution.py:94
  33.7 54.2 %all-gather.5.cloned.1.call-start = ((), (), s32[]{:S(2)}) async-start(), calls=%async_computation.8 | async-start | bytes 2621440 | tf_op jit(solution)/shard_map/all_gather | solution.py:43
  33.7 15.1 %copy-start.5 = (bf16[64,4096]{1,0:T(8,128)(2,1)S(1)}, bf16[64,4096]{1,0:T(8,128)(2,1)}, u32[]{:S(2)}) copy-start(bf16[64,4096]{1,0:T(8,128)(2,1)} %param.4) | copy-start | bytes 1572868
  48.8 4.6 %copy-start.6 = (bf16[64,4096]{1,0:T(8,128)(2,1)S(1)}, bf16[64,4096]{1,0:T(8,128)(2,1)}, u32[]{:S(2)}) copy-start(bf16[64,4096]{1,0:T(8,128)(2,1)} %param.7) | copy-start | bytes 1572868
  49.9 17.4 %all-to-all-start = ((bf16[64,4,8,128]{3,0,2,1:T(8,128)(2,1)}), bf16[64,4,8,128]{3,0,2,1:T(8,128)(2,1)S(1)}, u32[]{:S(2)}, u32[]{:S(2)}) async-start(bf16[64,4,8,128]{3,0,2,1:T(8,128)(2,1)} %copy.48), calls=%async_computation | async-start | bytes 1048576 | tf_op jit(solution)/shard_map/all_to_all | solution.py:92
  67.4 17.4 %all-to-all-start.4 = ((bf16[64,4,8,128]{3,0,2,1:T(8,128)(2,1)}), bf16[64,4,8,128]{3,0,2,1:T(8,128)(2,1)S(1)}, u32[]{:S(2)}, u32[]{:S(2)}) async-start(bf16[64,4,8,128]{3,0,2,1:T(8,128)(2,1)} %copy.59), calls=%async_computation.4 | async-start | bytes 1048576 | tf_op jit(solution)/shard_map/all_to_all | solution.py:95
  70.8 37.0 %all-gather.7.cloned.1.call-start = ((), (), s32[]{:S(2)}) async-start(), calls=%async_computation.9 | async-start | bytes 2621440 | tf_op jit(solution)/shard_map/all_gather | solution.py:44
  87.9 1.9 %copy-start.1 = (f32[8,128,256]{1,2,0:T(8,128)S(1)}, f32[8,128,256]{1,2,0:T(8,128)}, u32[]{:S(2)}) copy-start(f32[8,128,256]{1,2,0:T(8,128)} %convolution_bitcast_fusion.3) | copy-start | bytes 3145732
  91.3 20.3 %all-to-all-start.3 = ((bf16[256,1,8,128]{3,2,1,0:T(8,128)(2,1)}), bf16[256,1,8,128]{3,2,1,0:T(8,128)(2,1)}, u32[]{:S(2)}, u32[]{:S(2)}) async-start(bf16[256,1,8,128]{3,2,1,0:T(8,128)(2,1)} %copy.57), calls=%async_computation.3 | async-start | bytes 1048576 | tf_op jit(solution)/shard_map/all_to_all | solution.py:84
  96.9 12.8 %copy-start = (f32[8,128,256]{1,2,0:T(8,128)S(1)}, f32[8,128,256]{1,2,0:T(8,128)}, u32[]{:S(2)}) copy-start(f32[8,128,256]{1,2,0:T(8,128)} %convolution_bitcast_fusion) | copy-start | bytes 3145732
  109.7 0.7 copy-start.2
  111.6 19.6 %all-to-all-start.7 = ((bf16[256,1,8,128]{3,2,1,0:T(8,128)(2,1)}), bf16[256,1,8,128]{3,2,1,0:T(8,128)(2,1)}, u32[]{:S(2)}, u32[]{:S(2)}) async-start(bf16[256,1,8,128]{3,2,1,0:T(8,128)(2,1)} %copy.72), calls=%async_computation.7 | async-start | bytes 1048576 | tf_op jit(solution)/shard_map/all_to_all | solution.py:87
  116.2 0.9 copy-start.3
  131.2 17.5 %all-to-all-start.6 = ((bf16[256,1,8,128]{3,2,1,0:T(8,128)(2,1)}), bf16[256,1,8,128]{3,2,1,0:T(8,128)(2,1)S(1)}, u32[]{:S(2)}, u32[]{:S(2)}) async-start(bf16[256,1,8,128]{3,2,1,0:T(8,128)(2,1)} %copy.67), calls=%async_computation.6 | async-start | bytes 1048576 | tf_op jit(solution)/shard_map/all_to_all | solution.py:86
  148.7 17.4 %all-to-all-start.5 = ((bf16[256,1,8,128]{3,2,1,0:T(8,128)(2,1)}), bf16[256,1,8,128]{3,2,1,0:T(8,128)(2,1)S(1)}, u32[]{:S(2)}, u32[]{:S(2)}) async-start(bf16[256,1,8,128]{3,2,1,0:T(8,128)(2,1)} %copy.62), calls=%async_computation.5 | async-start | bytes 1048576 | tf_op jit(solution)/shard_map/all_to_all | solution.py:85
Sparse Core Ops, SparseCore 0:
  49.0 21.6 all-gather.4
  86.1 21.6 all-gather.6
where the time goes:
time: 175 us; the launch traced here: 174 us
  waiting for transfers between devices  98.2 us (56%)
  starting transfers between devices  32.5 us (19%)
  local copies, waits for them, and re-layouts  17.1 us (10%)
  between operations  14.3 us (8%)
  matrix products  8.12 us (5%)
  other arithmetic  3.83 us (2%)
    all_to_all x1, waiting for transfers between devices, shards(): lax.all_to_all(to_heads(value_rows), 'head', split_axis=1, concat_axis=0,...  13.9 us
    all_to_all x1, waiting for transfers between devices, shards(): lax.all_to_all(to_heads(out_grad), 'head', split_axis=1, concat_axis=0, t...  13.9 us
    all_to_all x1, waiting for transfers between devices, shards(): lax.all_to_all(to_heads(key_rows), 'head', split_axis=1, concat_axis=0, t...  13.4 us
    all_to_all x1, waiting for transfers between devices, shards(): lax.all_to_all(to_heads(queries), 'head', split_axis=1, concat_axis=0, ti...  12.8 us
    all_to_all x1, waiting for transfers between devices, per_head(): lax.all_to_all(results[3], 'head', split_axis=0, concat_axis=1, tiled=True)  12.6 us
    all_to_all x1, waiting for transfers between devices, per_head(): lax.all_to_all(results[2], 'head', split_axis=0, concat_axis=1, tiled=True)  12.1 us
    all_gather x1, waiting for transfers between devices, per_head(): lax.all_gather(grad_total[None], 'seq', axis=0, tiled=True)  10.9 us
    all_to_all x1, waiting for transfers between devices, per_head(): lax.all_to_all(results[1], 'head', split_axis=0, concat_axis=1, tiled=True)  8.53 us
  transfers between devices with their start and end apart: 10, of which 8 were waited for; matrix products, arithmetic and copies ran while one was open for 14% of the time, Pallas kernels for 0%

commit v1 on v0

--- a/solution.py
+++ b/solution.py
@@ -5,6 +5,18 @@
 
 DH = 128
 BLK_MAX = 512
+
+
+def sent_to_each(shard, axis, split, join):
+    ways, here = (lax.axis_size(axis), lax.axis_index(axis))
+    width = shard.shape[split] // ways
+    turned = jnp.roll(shard, -here * width, axis=split)
+    got = [lax.slice_in_dim(turned, 0, width, axis=split)]
+    for far in range(1, ways):
+        sent = lax.slice_in_dim(turned, far * width, (far + 1) * width, axis=split)
+        got.append(lax.ppermute(sent, axis, [(d, (d + far) % ways) for d in range(ways)]))
+    line = jnp.concatenate(got[::-1], axis=join)
+    return jnp.roll(line, (here + 1) * got[0].shape[join], axis=join)
 
 
 def shards(queries, key_rows, value_rows, out_grad):
@@ -92,7 +104,7 @@
             lax.all_to_all(to_heads(queries), "head", split_axis=1, concat_axis=0, tiled=True),
             lax.all_to_all(to_heads(key_rows), "head", split_axis=1, concat_axis=0, tiled=True),
             lax.all_to_all(to_heads(value_rows), "head", split_axis=1, concat_axis=0, tiled=True),
-            lax.all_to_all(to_heads(out_grad), "head", split_axis=1, concat_axis=0, tiled=True),
+            sent_to_each(to_heads(out_grad), "head", 1, 0),
         )
     )
     return tuple((item.reshape(tok_count, queries.shape[1]) for item in outputs))

time: 175 us -> 161 us (0.920)
  waiting for transfers between devices: 98.2 us -> 80.7 us
  matrix products: 8.12 us -> 10.7 us
    all_to_all x1 -> x0, waiting for transfers between devices: 13.9 us -> none  [shards(): lax.all_to_all(to_heads(out_grad), 'head', split_axis=1, concat_axis=0, t...]
    ppermute x0 -> x3, waiting for transfers between devices: none -> 12.1 us  [sent_to_each(): lax.ppermute(sent, axis, [(d, (d + far) % ways) for d in range(ways)])]
    all_to_all x1, waiting for transfers between devices: 0.01 us -> 11 us  [per_head(): lax.all_to_all(results[0], 'head', split_axis=0, concat_axis=1, tiled=True)]
    all_to_all x1, waiting for transfers between devices: 12.8 us -> 1.93 us  [shards(): lax.all_to_all(to_heads(queries), 'head', split_axis=1, concat_axis=0, ti...]
    all_gather x1, waiting for transfers between devices: 10.9 us -> 0.01 us  [per_head(): lax.all_gather(grad_total[None], 'seq', axis=0, tiled=True)]
    ppermute x0 -> x3, starting transfers between devices: none -> 3.48 us  [sent_to_each(): lax.ppermute(sent, axis, [(d, (d + far) % ways) for d in range(ways)])]
    all_to_all x1 -> x0, starting transfers between devices: 3.47 us -> none  [shards(): lax.all_to_all(to_heads(out_grad), 'head', split_axis=1, concat_axis=0, t...]
    all_to_all x1, waiting for transfers between devices: 12.6 us -> 9.56 us  [per_head(): lax.all_to_all(results[3], 'head', split_axis=0, concat_axis=1, tiled=True)]
  transfers between devices with their start and end apart: 10 -> 12, of which waited for: 8 -> 9; matrix products, arithmetic and copies ran while one was open for 14% -> 17% of each run, Pallas kernels for 0% -> 0%
where the time goes in v1:
time: 161 us; the launch traced here: 160 us
  waiting for transfers between devices  80.7 us (50%)
  starting transfers between devices  32.9 us (20%)
  local copies, waits for them, and re-layouts  16.9 us (10%)
  between operations  14.4 us (9%)
  matrix products  10.7 us (7%)
  other arithmetic  4.12 us (3%)
    all_to_all x1, waiting for transfers between devices, shards(): lax.all_to_all(to_heads(value_rows), 'head', split_axis=1, concat_axis=0,...  13.9 us
    all_to_all x1, waiting for transfers between devices, shards(): lax.all_to_all(to_heads(key_rows), 'head', split_axis=1, concat_axis=0, t...  13.4 us
    ppermute x3, waiting for transfers between devices, sent_to_each(): lax.ppermute(sent, axis, [(d, (d + far) % ways) for d in range(ways)])  12.1 us
    all_to_all x1, waiting for transfers between devices, per_head(): lax.all_to_all(results[0], 'head', split_axis=0, concat_axis=1, tiled=True)  11 us
    all_to_all x1, waiting for transfers between devices, per_head(): lax.all_to_all(results[2], 'head', split_axis=0, concat_axis=1, tiled=True)  11 us
    all_to_all x1, waiting for transfers between devices, per_head(): lax.all_to_all(results[3], 'head', split_axis=0, concat_axis=1, tiled=True)  9.56 us
    all_to_all x1, waiting for transfers between devices, per_head(): lax.all_to_all(results[1], 'head', split_axis=0, concat_axis=1, tiled=True)  7.98 us
    all_to_all x1, starting transfers between devices, shards(): lax.all_to_all(to_heads(key_rows), 'head', split_axis=1, concat_axis=0, t...  6.32 us
  transfers between devices with their start and end apart: 12, of which 9 were waited for; matrix products, arithmetic and copies ran while one was open for 17% of the time, Pallas kernels for 0%

profile of v1, /device:TPU:0, one launch (start us, length us, event | category | flops | bytes accessed | tf_op | source)
XLA Modules:
  0.0 159.8 jit_solution(10058954697166340036)
XLA Ops:
  7.2 1.2 copy.121
  8.4 1.0 copy.83
  9.4 6.3 %all-to-all-start.1 = ((bf16[64,4,8,128]{3,0,2,1:T(8,128)(2,1)}), bf16[64,4,8,128]{3,0,2,1:T(8,128)(2,1)S(1)}, u32[]{:S(2)}, u32[]{:S(2)}) async-start(bf16[64,4,8,128]{3,0,2,1:T(8,128)(2,1)} %copy.83), calls=%async_computation.1 | async-start | bytes 1048576 | tf_op jit(solution)/shard_map/all_to_all | solution.py:105
  15.7 0.1 copy.122
  15.8 1.0 copy.85
  16.8 13.4 %all-to-all-done.1 = bf16[64,4,8,128]{3,0,2,1:T(8,128)(2,1)S(1)} async-done(((bf16[64,4,8,128]{3,0,2,1:T(8,128)(2,1)}), bf16[64,4,8,128]{3,0,2,1:T(8,128)(2,1)S(1)}, u32[]{:S(2)}, u32[]{:S(2)}) %all-to-all-start.1) | async-done | bytes 524320 | tf_op jit(solution)/shard_map/all_to_all | solution.py:105
  30.2 3.5 %all-to-all-start.2 = ((bf16[64,4,8,128]{3,0,2,1:T(8,128)(2,1)}), bf16[64,4,8,128]{3,0,2,1:T(8,128)(2,1)S(1)}, u32[]{:S(2)}, u32[]{:S(2)}) async-start(bf16[64,4,8,128]{3,0,2,1:T(8,128)(2,1)} %copy.85), calls=%async_computation.2 | async-start | bytes 1048576 | tf_op jit(solution)/shard_map/all_to_all | solution.py:106
  33.7 0.0 all-gather.5.cloned.1.call-start
  33.7 0.0 copy-start.6
  33.8 13.9 %all-to-all-done.2 = bf16[64,4,8,128]{3,0,2,1:T(8,128)(2,1)S(1)} async-done(((bf16[64,4,8,128]{3,0,2,1:T(8,128)(2,1)}), bf16[64,4,8,128]{3,0,2,1:T(8,128)(2,1)S(1)}, u32[]{:S(2)}, u32[]{:S(2)}) %all-to-all-start.2) | async-done | bytes 524320 | tf_op jit(solution)/shard_map/all_to_all | solution.py:106
  47.7 1.1 fusion.29
  48.8 0.0 all-gather.5.cloned.1.call-update
  48.8 0.0 copy-start.7
  48.9 0.1 copy.123
  49.0 0.2 copy.92
  49.2 0.2 fusion.11
  49.4 0.7 fusion.28
  50.1 1.5 collective-permute-start
  51.6 0.0 collective-permute-start.1
  51.6 0.0 copy-done.7
  51.6 0.1 copy.120
  51.7 1.0 copy.81
  52.7 4.2 %all-to-all-start = ((bf16[64,4,8,128]{3,0,2,1:T(8,128)(2,1)}), bf16[64,4,8,128]{3,0,2,1:T(8,128)(2,1)S(1)}, u32[]{:S(2)}, u32[]{:S(2)}) async-start(bf16[64,4,8,128]{3,0,2,1:T(8,128)(2,1)} %copy.81), calls=%async_computation | async-start | bytes 1048576 | tf_op jit(solution)/shard_map/all_to_all | solution.py:104
  56.9 2.0 %collective-permute-start.2 = (bf16[64,1,8,128]{3,0,2,1:T(8,128)(2,1)}, bf16[64,1,8,128]{3,0,2,1:T(8,128)(2,1)S(1)}, u32[]{:S(2)}, u32[]{:S(2)}) collective-permute-start(bf16[64,1,8,128]{3,0,2,1:T(8,128)(2,1)} %get-tuple-element.4), channel_id=1, source_target_pairs={{0,1},{1,2},{2,3},{3,0},{4,5},{5,6},{6,7},{7,4},{8,9},{9,10},{10,1... | collective-permute-start | bytes 393224 | tf_op jit(solution)/shard_map/ppermute | solution.py:17
  58.9 0.0 collective-permute-done
  58.9 0.3 collective-permute-done.1
  59.3 11.7 %collective-permute-done.2 = bf16[64,1,8,128]{3,0,2,1:T(8,128)(2,1)S(1)} collective-permute-done((bf16[64,1,8,128]{3,0,2,1:T(8,128)(2,1)}, bf16[64,1,8,128]{3,0,2,1:T(8,128)(2,1)S(1)}, u32[]{:S(2)}, u32[]{:S(2)}) %collective-permute-start.2) | collective-permute-done | bytes 131104 | tf_op jit(solution)/shard_map/ppermute | solution.py:17
  71.2 1.9 %all-to-all-done = bf16[64,4,8,128]{3,0,2,1:T(8,128)(2,1)S(1)} async-done(((bf16[64,4,8,128]{3,0,2,1:T(8,128)(2,1)}), bf16[64,4,8,128]{3,0,2,1:T(8,128)(2,1)S(1)}, u32[]{:S(2)}, u32[]{:S(2)}) %all-to-all-start) | async-done | bytes 524320 | tf_op jit(solution)/shard_map/all_to_all | solution.py:104
  73.2 0.3 convolution_bitcast_fusion.3
  73.5 1.0 copy.99
  74.5 0.0 all-gather.7.cloned.1.call-update
  74.6 0.4 select_convert_fusion.1
  75.0 1.4 convolution_bitcast_fusion.2
  76.4 1.9 %multiply_reduce_fusion.1 = bf16[8,128,128]{2,1,0:T(8,128)(2,1)S(1)} fusion(f32[4,8,128,128]{3,2,1,0:T(8,128)} %bitcast.127, f32[4]{0:T(128)S(1)} %compare_convert_fusion.1), kind=kLoop, calls=%fused_computation.2 | loop fusion | flops 917504 | bytes 2359312 | tf_op jit(solution)/shard_map/reduce_sum | solution.py:62
  78.4 0.3 fusion.8
  78.7 1.1 copy.90
  79.8 4.3 %all-to-all-start.3 = ((bf16[256,1,8,128]{3,2,1,0:T(8,128)(2,1)}), bf16[256,1,8,128]{3,2,1,0:T(8,128)(2,1)S(1)}, u32[]{:S(2)}, u32[]{:S(2)}) async-start(bf16[256,1,8,128]{3,2,1,0:T(8,128)(2,1)} %copy.90), calls=%async_computation.3 | async-start | bytes 1048576 | tf_op jit(solution)/shard_map/all_to_all | solution.py:96
  84.1 1.6 select_convert_fusion
  85.7 0.4 convolution_bitcast_fusion.1
  86.2 0.3 fusion.10
  86.5 0.2 copy-done
  86.7 1.1 copy.95
  87.8 11.0 %all-to-all-done.3 = bf16[256,1,8,128]{3,2,1,0:T(8,128)(2,1)S(1)} async-done(((bf16[256,1,8,128]{3,2,1,0:T(8,128)(2,1)}), bf16[256,1,8,128]{3,2,1,0:T(8,128)(2,1)S(1)}, u32[]{:S(2)}, u32[]{:S(2)}) %all-to-all-start.3) | async-done | bytes 524320 | tf_op jit(solution)/shard_map/all_to_all | solution.py:96
  98.8 4.2 %all-to-all-start.4 = ((bf16[256,1,8,128]{3,2,1,0:T(8,128)(2,1)}), bf16[256,1,8,128]{3,2,1,0:T(8,128)(2,1)}, u32[]{:S(2)}, u32[]{:S(2)}) async-start(bf16[256,1,8,128]{3,2,1,0:T(8,128)(2,1)} %copy.95), calls=%async_computation.4 | async-start | bytes 1048576 | tf_op jit(solution)/shard_map/all_to_all | solution.py:97
  103.0 2.7 %convolution_bitcast_fusion = f32[8,128,256]{1,2,0:T(8,128)} fusion(bf16[8,256,256]{2,1,0:T(8,128)(2,1)} %copy-done, bf16[256,8,128]{2,0,1:T(8,128)(2,1)S(1)} %bitcast.126), kind=kOutput, calls=%fused_computation.12 | convolution fusion | flops 134217728 | bytes 2621440 | tf_op jit(solution)/shard_map/bhts,bthd->bshd/dot_general | solution.py:81
  105.6 1.9 %multiply_reduce_fusion = bf16[8,128,128]{2,1,0:T(8,128)(2,1)S(1)} fusion(f32[4,8,128,128]{3,2,1,0:T(8,128)} %bitcast.128, f32[4]{0:T(128)S(1)} %compare_convert_fusion), kind=kLoop, calls=%fused_computation | loop fusion | flops 917504 | bytes 2359312 | tf_op jit(solution)/shard_map/reduce_sum | solution.py:63
  107.6 0.3 fusion.9
  107.9 1.1 copy.101
  109.0 8.0 %all-to-all-done.4 = bf16[256,1,8,128]{3,2,1,0:T(8,128)(2,1)} async-done(((bf16[256,1,8,128]{3,2,1,0:T(8,128)(2,1)}), bf16[256,1,8,128]{3,2,1,0:T(8,128)(2,1)}, u32[]{:S(2)}, u32[]{:S(2)}) %all-to-all-start.4) | async-done | bytes 524320 | tf_op jit(solution)/shard_map/all_to_all | solution.py:97
  117.0 3.5 %all-to-all-start.5 = ((bf16[256,1,8,128]{3,2,1,0:T(8,128)(2,1)}), bf16[256,1,8,128]{3,2,1,0:T(8,128)(2,1)S(1)}, u32[]{:S(2)}, u32[]{:S(2)}) async-start(bf16[256,1,8,128]{3,2,1,0:T(8,128)(2,1)} %copy.101), calls=%async_computation.5 | async-start | bytes 1048576 | tf_op jit(solution)/shard_map/all_to_all | solution.py:98
  120.5 0.3 convolution_multiply_fusion
  120.8 1.6 fusion.7
  122.4 1.1 copy.107
  123.5 11.0 %all-to-all-done.5 = bf16[256,1,8,128]{3,2,1,0:T(8,128)(2,1)S(1)} async-done(((bf16[256,1,8,128]{3,2,1,0:T(8,128)(2,1)}), bf16[256,1,8,128]{3,2,1,0:T(8,128)(2,1)S(1)}, u32[]{:S(2)}, u32[]{:S(2)}) %all-to-all-start.5) | async-done | bytes 524320 | tf_op jit(solution)/shard_map/all_to_all | solution.py:98
  134.5 3.5 %all-to-all-start.6 = ((bf16[256,1,8,128]{3,2,1,0:T(8,128)(2,1)}), bf16[256,1,8,128]{3,2,1,0:T(8,128)(2,1)S(1)}, u32[]{:S(2)}, u32[]{:S(2)}) async-start(bf16[256,1,8,128]{3,2,1,0:T(8,128)(2,1)} %copy.107), calls=%async_computation.6 | async-start | bytes 1048576 | tf_op jit(solution)/shard_map/all_to_all | solution.py:99
  137.9 0.1 copy.91
  138.0 1.0 reshape.186
  139.1 1.1 copy.96
  140.2 1.0 reshape.190
  141.2 0.1 copy.102
  141.3 1.0 reshape.192
  142.3 9.6 %all-to-all-done.6 = bf16[256,1,8,128]{3,2,1,0:T(8,128)(2,1)S(1)} async-done(((bf16[256,1,8,128]{3,2,1,0:T(8,128)(2,1)}), bf16[256,1,8,128]{3,2,1,0:T(8,128)(2,1)S(1)}, u32[]{:S(2)}, u32[]{:S(2)}) %all-to-all-start.6) | async-done | bytes 524320 | tf_op jit(solution)/shard_map/all_to_all | solution.py:99
  151.9 0.1 copy.108
  152.0 1.0 reshape.194
  (29 shorter events, 0.3 us)
Async XLA Ops:
  7.2 8.5 %copy-start.5 = (bf16[64,4096]{1,0:T(8,128)(2,1)S(1)}, bf16[64,4096]{1,0:T(8,128)(2,1)}, u32[]{:S(2)}) copy-start(bf16[64,4096]{1,0:T(8,128)(2,1)} %param.6) | copy-start | bytes 1572868
  9.4 20.8 %all-to-all-start.1 = ((bf16[64,4,8,128]{3,0,2,1:T(8,128)(2,1)}), bf16[64,4,8,128]{3,0,2,1:T(8,128)(2,1)S(1)}, u32[]{:S(2)}, u32[]{:S(2)}) async-start(bf16[64,4,8,128]{3,0,2,1:T(8,128)(2,1)} %copy.83), calls=%async_computation.1 | async-start | bytes 1048576 | tf_op jit(solution)/shard_map/all_to_all | solution.py:105
  30.2 17.4 %all-to-all-start.2 = ((bf16[64,4,8,128]{3,0,2,1:T(8,128)(2,1)}), bf16[64,4,8,128]{3,0,2,1:T(8,128)(2,1)S(1)}, u32[]{:S(2)}, u32[]{:S(2)}) async-start(bf16[64,4,8,128]{3,0,2,1:T(8,128)(2,1)} %copy.85), calls=%async_computation.2 | async-start | bytes 1048576 | tf_op jit(solution)/shard_map/all_to_all | solution.py:106
  33.7 42.8 %all-gather.5.cloned.1.call-start = ((), (), s32[]{:S(2)}) async-start(), calls=%async_computation.7 | async-start | bytes 2621440 | tf_op jit(solution)/shard_map/all_gather | solution.py:55
  33.7 15.2 %copy-start.6 = (bf16[64,4096]{1,0:T(8,128)(2,1)S(1)}, bf16[64,4096]{1,0:T(8,128)(2,1)}, u32[]{:S(2)}) copy-start(bf16[64,4096]{1,0:T(8,128)(2,1)} %param.7) | copy-start | bytes 1572868
  48.8 2.8 %copy-start.7 = (bf16[64,4096]{1,0:T(8,128)(2,1)S(1)}, bf16[64,4096]{1,0:T(8,128)(2,1)}, u32[]{:S(2)}) copy-start(bf16[64,4096]{1,0:T(8,128)(2,1)} %param.4) | copy-start | bytes 1572868
  50.1 8.8 %collective-permute-start = (bf16[64,1,8,128]{3,0,2,1:T(8,128)(2,1)S(1)}, bf16[64,1,8,128]{3,0,2,1:T(8,128)(2,1)S(1)}, u32[]{:S(2)}, u32[]{:S(2)}) collective-permute-start(bf16[64,1,8,128]{3,0,2,1:T(8,128)(2,1)S(1)} %get-tuple-element.6), channel_id=1, source_target_pairs={{0,3},{1,0},{2,1},{3,2},{4,7},{5,4},{6,5},{7,6},{8,11},{9,8},{10,9... | collective-permute-start | bytes 393224 | tf_op jit(solution)/shard_map/ppermute | solution.py:17
  51.6 7.7 %collective-permute-start.1 = (bf16[64,1,8,128]{3,0,2,1:T(8,128)(2,1)}, bf16[64,1,8,128]{3,0,2,1:T(8,128)(2,1)S(1)}, u32[]{:S(2)}, u32[]{:S(2)}) collective-permute-start(bf16[64,1,8,128]{3,0,2,1:T(8,128)(2,1)} %get-tuple-element.5), channel_id=1, source_target_pairs={{0,2},{1,3},{2,0},{3,1},{4,6},{5,7},{6,4},{7,5},{8,10},{9,11},{10,... | collective-permute-start | bytes 393224 | tf_op jit(solution)/shard_map/ppermute | solution.py:17
  52.7 20.4 %all-to-all-start = ((bf16[64,4,8,128]{3,0,2,1:T(8,128)(2,1)}), bf16[64,4,8,128]{3,0,2,1:T(8,128)(2,1)S(1)}, u32[]{:S(2)}, u32[]{:S(2)}) async-start(bf16[64,4,8,128]{3,0,2,1:T(8,128)(2,1)} %copy.81), calls=%async_computation | async-start | bytes 1048576 | tf_op jit(solution)/shard_map/all_to_all | solution.py:104
  56.9 48.7 %all-gather.7.cloned.1.call-start = ((), (), s32[]{:S(2)}) async-start(), calls=%async_computation.8 | async-start | bytes 2621440 | tf_op jit(solution)/shard_map/all_gather | solution.py:56
  56.9 14.1 %collective-permute-start.2 = (bf16[64,1,8,128]{3,0,2,1:T(8,128)(2,1)}, bf16[64,1,8,128]{3,0,2,1:T(8,128)(2,1)S(1)}, u32[]{:S(2)}, u32[]{:S(2)}) collective-permute-start(bf16[64,1,8,128]{3,0,2,1:T(8,128)(2,1)} %get-tuple-element.4), channel_id=1, source_target_pairs={{0,1},{1,2},{2,3},{3,0},{4,5},{5,6},{6,7},{7,4},{8,9},{9,10},{10,1... | collective-permute-start | bytes 393224 | tf_op jit(solution)/shard_map/ppermute | solution.py:17
  71.2 3.4 %copy-start.3 = (bf16[512,1,8,128]{3,0,2,1:T(8,128)(2,1)}, bf16[512,1,8,128]{3,0,2,1:T(8,128)(2,1)S(1)}, u32[]{:S(2)}) copy-start(bf16[512,1,8,128]{3,0,2,1:T(8,128)(2,1)S(1)} %slice_dynamic-update-slice_fusion.1) | copy-start | bytes 3145732
  76.4 1.9 %copy-start.2 = (f32[8,128,256]{1,2,0:T(8,128)S(1)}, f32[8,128,256]{1,2,0:T(8,128)}, u32[]{:S(2)}) copy-start(f32[8,128,256]{1,2,0:T(8,128)} %convolution_bitcast_fusion.2) | copy-start | bytes 3145732
  79.8 19.0 %all-to-all-start.3 = ((bf16[256,1,8,128]{3,2,1,0:T(8,128)(2,1)}), bf16[256,1,8,128]{3,2,1,0:T(8,128)(2,1)S(1)}, u32[]{:S(2)}, u32[]{:S(2)}) async-start(bf16[256,1,8,128]{3,2,1,0:T(8,128)(2,1)} %copy.90), calls=%async_computation.3 | async-start | bytes 1048576 | tf_op jit(solution)/shard_map/all_to_all | solution.py:96
  84.1 2.0 %copy-start.4 = (bf16[512,1,8,128]{3,0,2,1:T(8,128)(2,1)S(1)}, bf16[512,1,8,128]{3,0,2,1:T(8,128)(2,1)}, u32[]{:S(2)}) copy-start(bf16[512,1,8,128]{3,0,2,1:T(8,128)(2,1)} %copy-done.3) | copy-start | bytes 3145732
  85.7 1.0 copy-start
  98.8 18.2 %all-to-all-start.4 = ((bf16[256,1,8,128]{3,2,1,0:T(8,128)(2,1)}), bf16[256,1,8,128]{3,2,1,0:T(8,128)(2,1)}, u32[]{:S(2)}, u32[]{:S(2)}) async-start(bf16[256,1,8,128]{3,2,1,0:T(8,128)(2,1)} %copy.95), calls=%async_computation.4 | async-start | bytes 1048576 | tf_op jit(solution)/shard_map/all_to_all | solution.py:97
  105.6 1.9 %copy-start.1 = (f32[8,128,256]{1,2,0:T(8,128)S(1)}, f32[8,128,256]{1,2,0:T(8,128)}, u32[]{:S(2)}) copy-start(f32[8,128,256]{1,2,0:T(8,128)} %convolution_bitcast_fusion) | copy-start | bytes 3145732
  117.0 17.4 %all-to-all-start.5 = ((bf16[256,1,8,128]{3,2,1,0:T(8,128)(2,1)}), bf16[256,1,8,128]{3,2,1,0:T(8,128)(2,1)S(1)}, u32[]{:S(2)}, u32[]{:S(2)}) async-start(bf16[256,1,8,128]{3,2,1,0:T(8,128)(2,1)} %copy.101), calls=%async_computation.5 | async-start | bytes 1048576 | tf_op jit(solution)/shard_map/all_to_all | solution.py:98
  134.5 17.4 %all-to-all-start.6 = ((bf16[256,1,8,128]{3,2,1,0:T(8,128)(2,1)}), bf16[256,1,8,128]{3,2,1,0:T(8,128)(2,1)S(1)}, u32[]{:S(2)}, u32[]{:S(2)}) async-start(bf16[256,1,8,128]{3,2,1,0:T(8,128)(2,1)} %copy.107), calls=%async_computation.6 | async-start | bytes 1048576 | tf_op jit(solution)/shard_map/all_to_all | solution.py:99
Sparse Core Ops, SparseCore 0:
  49.0 21.6 all-gather.4
  74.7 23.2 all-gather.6
